TPU v7x, 512 devices: a whole 4x8x8 slice. The times are simulated.
512 devices in a mesh: fsdp: 32 (over y, x), tensor: 16 (over z, core).
Axes of the slice: x: 4, y: 8, z: 8, core: 2. Of those that a mesh axis runs over, the one named last changes fastest.
Arguments:
- inputs: bfloat16 [8192, 8192], P('tensor', 'fsdp'), may hold values from -6 to 6
- grad_out: bfloat16 [8192, 8192], P('fsdp', 'tensor'), may hold values from -0.0625 to 0.0625
- filters: bfloat16 [512, 128], P('tensor'), may hold values from -0.5 to 0.5
- momentum: float32 [8192, 8192], P('fsdp', 'tensor'), may hold values from -6 to 6
- basis: float32 [8192, 256], P('tensor'), may hold values from -6 to 6
Outputs:
- update: bfloat16 [8192, 8192], P('fsdp', 'tensor')
- new_momentum: float32 [8192, 8192], P('fsdp', 'tensor')
- new_basis: float32 [8192, 256], P('tensor')
All inputs are finite; a program needn't handle non-finite values.
Results may differ from a plain program's by a relative error of at most 0.0051.
Values may be sent and summed in bfloat16 or wider, within the bound.
A program may use at most 64 MiB of HBM per device.

v0:
```python
import math

import jax
import jax.numpy as jnp
from jax import lax
from jax.sharding import PartitionSpec as P

D = 8192
GROUP = 16
RANK = 256


momentum_decay = 0.95
epsilon = 1e-06


def passed_along(block, axis, distance):
    devices = range(lax.axis_size(axis))
    route = [(i - distance, i) for i in devices if i - distance in devices]
    return lax.ppermute(block, axis, route)


def toeplitz(filters, taps):
    rows_out = lax.broadcasted_iota(jnp.int32, (taps, 2 * taps), 0)
    cols_in = lax.broadcasted_iota(jnp.int32, (taps, 2 * taps), 1)
    offset = cols_in - rows_out
    valid = (offset >= 0) & (offset < taps)
    picked = jnp.take(filters, jnp.clip(offset, 0, taps - 1), axis=1)
    return jnp.where(valid[None], picked, jnp.zeros_like(picked))


def convolve(grad_out, tail_rows, filters):
    tokens_here, channels = grad_out.shape
    taps = filters.shape[1]
    extended = jnp.concatenate(
        [grad_out, tail_rows, jnp.zeros((1, channels), grad_out.dtype)], axis=0
    )
    blocks = extended.reshape(tokens_here // taps + 1, taps, channels // GROUP, GROUP)
    windows = jnp.concatenate([blocks[:-1], blocks[1:]], axis=1)
    matrix = toeplitz(filters, taps)
    result = jnp.einsum("gas,bsgc->bagc", matrix, windows, preferred_element_type=jnp.float32)
    return result.reshape(tokens_here, channels).astype(jnp.bfloat16)


def contract_rows(left_side, right_hand):
    return lax.dot_general(
        left_side,
        right_hand,
        (((0,), (0,)), ((), ())),
        precision=lax.Precision.HIGHEST,
        preferred_element_type=jnp.float32,
    )


def orthonormalize(sketch_rows, gram_matrix):
    factor = jnp.linalg.cholesky(gram_matrix)
    return jax.scipy.linalg.solve_triangular(factor, sketch_rows.T, lower=True).T


def shards(inputs, grad_out, filters, momentum, basis):
    highest = lax.Precision.HIGHEST
    taps = filters.shape[1]
    tail_rows = passed_along(grad_out[: taps - 1], "fsdp", -1)
    grad_mixed = convolve(grad_out, tail_rows, filters)
    input_cols = lax.all_gather(inputs, "tensor", axis=0, tiled=True)
    gradient = lax.dot_general(
        input_cols,
        lax.all_gather(grad_mixed, "fsdp", axis=0, tiled=True),
        (((0,), (0,)), ((), ())),
        preferred_element_type=jnp.float32,
    )
    blended = momentum + gradient
    partial_sketch = jnp.dot(blended, basis, precision=highest)
    sketch = lax.psum(partial_sketch, "tensor")
    gram_matrix = lax.psum(contract_rows(sketch, sketch), "fsdp")
    orthonormal = orthonormalize(sketch, gram_matrix)
    partial_right = contract_rows(blended, orthonormal)
    projected = lax.psum(partial_right, "fsdp")
    squares = lax.psum(jnp.sum(projected * projected, axis=0), "tensor")
    new_basis = projected / jnp.sqrt(squares / D + epsilon)
    new_momentum = blended - (1.0 - momentum_decay) * jnp.dot(
        orthonormal, projected.T, precision=highest
    )
    update = (math.sqrt(D / RANK) * jnp.dot(orthonormal, new_basis.T, precision=highest)).astype(
        jnp.bfloat16
    )
    return (update, new_momentum, new_basis)


def solution(mesh):
    placed = (
        P("tensor", "fsdp"),
        P("fsdp", "tensor"),
        P("tensor", None),
        P("fsdp", "tensor"),
        P("tensor", None),
    )
    return jax.shard_map(
        shards,
        mesh=mesh,
        in_specs=placed,
        out_specs=(P("fsdp", "tensor"), P("fsdp", "tensor"), P("tensor", None)),
        check_vma=False,
    )
```

profile of v0, /device:TPU:1, one launch (start us, length us, event | category | flops | bytes accessed | tf_op | source)
XLA Modules:
  0.0 794.0 jit_solution(10221885347929351109)
XLA Ops:
  8.9 1.3 collective-permute-start
  12.2 114.2 %gather_fusion = bf16[32768,32]{1,0:T(8,128)(2,1)} fusion(bf16[32,128]{0,1:T(8,128)(2,1)S(1)} %copy.19, s32[32768]{0:T(1024)S(1)} %broadcast_clamp_fusion), kind=kCustom, calls=%fused_computation | custom fusion | bytes 4325376 | tf_op jit(solution)/shard_map/jit(_take)/gather | solution.py:28
  126.4 7.5 copy.20
  136.2 1.8 fusion.12
  139.0 1.2 copy.22
  140.2 111.9 %all-gather.3.cloned.1.call-done = bf16[8192,512]{0,1:T(8,128)(2,1)} async-done(((bf16[256,512]{0,1:T(8,128)(2,1)}), bf16[8192,512]{0,1:T(8,128)(2,1)}) %all-gather.3.cloned.1.call-update) | async-done | bytes 8388624 | tf_op jit(solution)/shard_map/all_gather | solution.py:68
  252.1 6.9 fusion.7
  259.1 1.7 fusion.44
  260.8 115.5 %all-reduce.5.cloned.1.call-done = f32[256,256]{1,0:T(8,128)} async-done(((f32[256,256]{1,0:T(8,128)}), f32[256,256]{1,0:T(8,128)}) %all-reduce.5.cloned.1.call-update) | async-done | bytes 262160 | tf_op jit(solution)/shard_map/psum | solution.py:74
  376.3 2.4 fusion.45
  379.0 152.1 %all-reduce.7.cloned.1.call-done = f32[256,256]{0,1:T(8,128)} async-done(((f32[256,256]{0,1:T(8,128)}), f32[256,256]{0,1:T(8,128)}) %all-reduce.7.cloned.1.call-update) | async-done | bytes 262160 | tf_op jit(solution)/shard_map/psum | solution.py:75
  533.2 11.7 %cholesky.50 = f32[128,128]{1,0:T(8,128)S(1)} custom-call(f32[128,128]{1,0:T(8,128)S(1)} %cholesky.118), custom_call_target="Cholesky" | custom-call | tf_op jit(solution)/shard_map/jit(cholesky)/cholesky | solution.py:56
  544.9 9.8 %custom-call.15 = f32[1,128,128]{1,2,0:T(8,128)S(1)} custom-call(f32[1,128,128]{2,1,0:T(8,128)S(1)} %get-tuple-element.30), custom_call_target="InvertDiagBlocksLowerTriangular" | custom-call | tf_op jit(solution)/shard_map/jit(cholesky)/cholesky | solution.py:56
  555.2 11.7 %cholesky.105 = f32[128,128]{1,0:T(8,128)S(1)} custom-call(f32[128,128]{1,0:T(8,128)S(1)} %convolution_subtract_fusion.1), custom_call_target="Cholesky" | custom-call | tf_op jit(solution)/shard_map/jit(cholesky)/cholesky | solution.py:56
  569.7 4.2 while.1
  570.4 1.4 bitcast_dynamic-update-slice_fusion.2
  572.4 1.4 bitcast_dynamic-update-slice_fusion.2
  573.8 19.7 %custom-call.16 = f32[2,128,128]{1,2,0:T(8,128)S(1)} custom-call(f32[2,128,128]{2,1,0:T(8,128)S(1)} %get-tuple-element.10), custom_call_target="InvertDiagBlocksLowerTriangular" | custom-call | tf_op jit(solution)/shard_map/jit(_solve_triangular)/triangular_solve | solution.py:57
  594.6 1.4 fusion.22
  596.0 155.6 %all-reduce.9.cloned.1.call-done = f32[512,256]{1,0:T(8,128)} async-done(((f32[512,256]{1,0:T(8,128)}), f32[512,256]{1,0:T(8,128)}) %all-reduce.9.cloned.1.call-update) | async-done | bytes 524304 | tf_op jit(solution)/shard_map/psum | solution.py:78
  751.6 1.6 fusion.6
  754.3 1.1 multiply_reduce_fusion
  755.4 29.2 %psum.31 = f32[256]{0:T(256)S(1)} all-reduce(f32[256]{0:T(256)S(1)} %multiply_reduce_fusion), channel_id=1, replica_groups=mesh['fsdp'=32,'tensor'=16] {'tensor'}, use_global_device_ids=true, to_apply=%region_8.9 | all-reduce | flops 256 | bytes 2048 | tf_op jit(solution)/shard_map/psum | solution.py:79
  785.7 1.8 fusion.8
  (61 shorter events, 15.6 us)
Async XLA Ops:
  7.2 251.9 %copy-start = (f32[512,256]{1,0:T(8,128)S(1)}, f32[512,256]{1,0:T(8,128)}, u32[]{:S(2)}) copy-start(f32[512,256]{1,0:T(8,128)} %param.9) | copy-start | bytes 1572868
  7.2 133.1 %all-gather.5.cloned.1.call-start = ((), (), s32[]{:S(2)}) async-start(), calls=%async_computation.1 | async-start | bytes 4456448 | tf_op jit(solution)/shard_map/all_gather | solution.py:65
  7.9 244.2 %all-gather.3.cloned.1.call-start = ((), (), s32[]{:S(2)}) async-start(), calls=%async_computation | async-start | bytes 8650752 | tf_op jit(solution)/shard_map/all_gather | solution.py:68
  8.9 126.0 %collective-permute-start = (bf16[127,512]{1,0:T(8,128)(2,1)S(1)}, bf16[127,512]{1,0:T(8,128)(2,1)}, u32[]{:S(2)}, u32[]{:S(2)}) collective-permute-start(bf16[127,512]{1,0:T(8,128)(2,1)S(1)} %slice.61), channel_id=1, source_target_pairs={{16,0},{32,16},{48,32},{64,48},{80,64},{96,80},{112,96},{128,112},... | collective-permute-start | bytes 390152 | tf_op jit(solution)/shard_map/ppermute | solution.py:20
  126.4 8.5 %copy-start.3 = (bf16[256,512]{1,0:T(8,128)(2,1)S(1)}, bf16[256,512]{1,0:T(8,128)(2,1)}, u32[]{:S(2)}) copy-start(bf16[256,512]{1,0:T(8,128)(2,1)} %param.6) | copy-start | bytes 786436
  138.9 237.4 %all-reduce.5.cloned.1.call-start = ((), (), s32[]{:S(2)}) async-start(), calls=%async_computation.2 | async-start | bytes 524288 | tf_op jit(solution)/shard_map/psum | solution.py:74
  260.8 270.3 %all-reduce.7.cloned.1.call-start = ((), (), s32[]{:S(2)}) async-start(), calls=%async_computation.3 | async-start | bytes 524288 | tf_op jit(solution)/shard_map/psum | solution.py:75
  376.3 217.2 %copy-start.1 = (f32[256,256]{1,0:T(8,128)S(1)}, f32[256,256]{1,0:T(8,128)}, u32[]{:S(2)}) copy-start(f32[256,256]{1,0:T(8,128)} %all-reduce.5.cloned.1.call-done) | copy-start | bytes 786436
  378.7 372.9 %all-reduce.9.cloned.1.call-start = ((), (), s32[]{:S(2)}) async-start(), calls=%async_computation.4 | async-start | bytes 1048576 | tf_op jit(solution)/shard_map/psum | solution.py:78
  785.7 1.8 copy-start.2
Sparse Core Ops, SparseCore 0:
  10.1 51.5 all-gather.4
  139.0 113.0 all-gather.2
  260.9 115.3 all-reduce.4
  380.6 150.4 all-reduce.6
  596.1 155.4 all-reduce.8
where the time goes:
time: 795 us; the launch traced here: 794 us
  waiting for transfers between devices  536 us (67%)
  local copies, waits for them, and re-layouts  134 us (17%)
  other arithmetic  58.7 us (7%)
  blocking collectives  29.2 us (4%)
  matrix products  19 us (2%)
  between operations  15.4 us (2%)
    psum x1, waiting for transfers between devices, shards(): projected = lax.psum(partial_right, 'fsdp')  156 us
    psum x1, waiting for transfers between devices, shards(): gram_matrix = lax.psum(contract_rows(sketch, sketch), 'fsdp')  152 us
    gather x2, local copies, waits for them, and re-layouts, toeplitz(): picked = jnp.take(filters, jnp.clip(offset, 0, taps - 1), axis=1)  122 us
    psum x1, waiting for transfers between devices, shards(): sketch = lax.psum(partial_sketch, 'tensor')  115 us
    all_gather x1, waiting for transfers between devices, shards(): lax.all_gather(grad_mixed, 'fsdp', axis=0, tiled=True)  112 us
    another operation x7, other arithmetic, orthonormalize(): factor = jnp.linalg.cholesky(gram_matrix)  34.6 us
    psum x1, blocking collectives, shards(): squares = lax.psum(jnp.sum(projected * projected, axis=0), 'tensor')  29.2 us
    another operation x3, other arithmetic, orthonormalize(): jax.scipy.linalg.solve_triangular(factor, sketch_rows.T, lower=True)  19.7 us
  transfers between devices with their start and end apart: 6, of which 4 were waited for; matrix products, arithmetic and copies ran while one was open for 16% of the time, Pallas kernels for 0%

commit v1 on v0

v1 whole, which is shorter than its diff:
```python
import functools
import math

import jax
import jax.numpy as jnp
from jax import lax
from jax.experimental import pallas as pl
from jax.experimental.pallas import tpu as pltpu
from jax.sharding import PartitionSpec as P

D = 8192
GROUP = 16
RANK = 256
TAPS = 128
HALF = 128

momentum_decay = 0.95
epsilon = 1e-06

MESH = pl.DeviceIdType.MESH
HIGHEST = lax.Precision.HIGHEST
VMEM = pl.BlockSpec(memory_space=pltpu.VMEM)


class Place:
    def __init__(self, sizes):
        self.X, self.Y, self.Z = sizes
        self.F, self.T = self.X * self.Y, self.Z * 2
        self.f, self.t = lax.axis_index("fsdp"), lax.axis_index("tensor")
        self.y, self.x = self.f // self.X, lax.rem(self.f, self.X)
        self.z, self.c = self.t // 2, lax.rem(self.t, 2)

    def wrap(self, value, n):
        return lax.rem(value + 2 * n, n)

    def plane(self, dy, dx):
        return (self.wrap(self.y + dy, self.Y) * self.X + self.wrap(self.x + dx, self.X), self.t)

    def along_z(self, dz):
        return (self.f, self.wrap(self.z + dz, self.Z) * 2 + self.c)

    def sibling(self):
        return (self.f, self.z * 2 + 1 - self.c)

    def fsdp(self, d):
        return (self.wrap(self.f + d, self.F), self.t)

    def tensor(self, d):
        return (self.f, self.wrap(self.t + d, self.T))


def greet(peers):
    barrier = pltpu.get_barrier_semaphore()
    for peer in peers:
        pl.semaphore_signal(barrier, inc=1, device_id=peer, device_id_type=MESH)


def all_greeted(peers):
    pl.semaphore_wait(pltpu.get_barrier_semaphore(), len(peers))


def remote(src, dst, send, recv, peer):
    return pltpu.make_async_remote_copy(
        src_ref=src, dst_ref=dst, send_sem=send, recv_sem=recv, device_id=peer, device_id_type=MESH
    )


def ring(n, axis, rows, tell, first):
    lo, count = rows
    half = n // 2
    pieces = [(0, rows, first)]
    for sign in (1, -1):
        before = first
        for step in range(1, half + 1):
            part = rows
            if step == half:
                part = (lo, count // 2) if sign > 0 else (lo + count // 2, count // 2)
            before = tell(axis, sign, sign * (step - 1), part, before)
            pieces.append((sign * step, part, before))
    return pieces


def plan(sizes):
    X, Y, Z = sizes
    messages = []

    def teller(part, fixed):
        def tell(axis, sign, offset, rows, needs):
            where = dict(fixed)
            where[axis] = offset
            messages.append(dict(part=part, axis=axis, sign=sign, at=where, rows=rows, needs=needs))
            return len(messages) - 1

        return tell

    for ox, rows, needs in ring(X, "x", (0, HALF), teller("A", {"y": 0}), "A"):
        ring(Y, "y", rows, teller("A", {"x": ox}), needs)
    for oy, rows, needs in ring(Y, "y", (0, HALF), teller("B", {"x": 0}), "B"):
        ring(X, "x", rows, teller("B", {"y": oy}), needs)
    for oz, rows, needs in ring(Z, "z", (0, 256), teller("I", {}), "I"):
        teller("I", {"z": oz})("c", 1, 0, rows, needs)
    ready = {"I": 0.5, "B": 1.5, "A": 5.0}
    free, arrival = {}, {}
    waiting = list(range(len(messages)))
    while waiting:
        when = {m: ready[messages[m]["needs"]] for m in waiting if messages[m]["needs"] in ready}
        best = min(when, key=lambda m: (max(when[m], free.get((messages[m]["axis"], messages[m]["sign"]), 0)), when[m], m))
        message = messages[best]
        link = (message["axis"], message["sign"])
        start = max(when[best], free.get(link, 0.0))
        length = message["rows"][1] * 1024 * (2 / 1e5 if link[0] != "c" else 1 / 4e5)
        free[link] = start + length
        ready[best] = arrival[best] = start + length + 1.8
        message["starts"] = start
        waiting.remove(best)
    order = sorted(arrival, key=lambda m: arrival[m])
    return messages, order, arrival


def strided_taps(filters, toeplitz_ref):
    count = filters.shape[0]
    wide = jnp.concatenate([filters, jnp.zeros_like(filters)], axis=1)
    for g in range(count):
        rows = jnp.broadcast_to(wide[g : g + 1, :], (TAPS, 2 * TAPS))
        rolled = pltpu.roll(rows, 0, 1, stride=1, stride_axis=0)
        toeplitz_ref[g * TAPS : (g + 1) * TAPS, :] = rolled.astype(jnp.bfloat16)


def convolve(toeplitz_ref, window):
    channels = window.shape[1]
    group = lax.broadcasted_iota(jnp.int32, (TAPS, 128), 1) // GROUP
    each = 128 // GROUP
    columns = []
    for q in range(channels // 128):
        product = jnp.dot(
            toeplitz_ref[q * each * TAPS : (q + 1) * each * TAPS, :],
            window[:, q * 128 : (q + 1) * 128],
            preferred_element_type=jnp.float32,
        )
        total = product[:TAPS]
        for i in range(1, each):
            total = jnp.where(group == i, product[i * TAPS : (i + 1) * TAPS], total)
        columns.append(total)
    return jnp.concatenate(columns, axis=1).astype(jnp.bfloat16)


def gather_kernel(
    sizes, inputs_ref, grad_ref, filters_ref, momentum_ref, basis_ref, blended_ref, sketch_ref,
    halo, toeplitz, first, second, features, halo_sem, send_sem, recv_sem,
):
    me = Place(sizes)
    peers = [me.plane(0, 1), me.plane(0, -1), me.plane(1, 0), me.plane(-1, 0)]
    peers += [me.along_z(1), me.along_z(-1), me.sibling(), me.fsdp(1), me.fsdp(-1)]
    greet(peers)
    messages, order, _ = plan(sizes)
    strided_taps(filters_ref[...].astype(jnp.float32), toeplitz)
    features[me.t] = jnp.transpose(inputs_ref[...].astype(jnp.float32)).astype(jnp.bfloat16)
    all_greeted(peers)

    def copy_of(m, arriving):
        message = messages[m]
        sign = message["sign"]
        shift = sign if arriving else 0
        at, axis = dict(message["at"]), message["axis"]
        rows = pl.ds(*message["rows"])
        if axis in at:
            at[axis] += shift
        if message["part"] == "I":
            core = me.c
            if axis == "c" and arriving:
                core = 1 - me.c
            block = features.at[me.wrap(me.z - at["z"], me.Z) * 2 + core, rows]
            peer = me.sibling() if axis == "c" else me.along_z(sign)
        else:
            y, x = me.wrap(me.y - at["y"], me.Y), me.wrap(me.x - at["x"], me.X)
            block = second.at[y, x, rows] if message["part"] == "A" else first.at[x, y, rows]
            peer = me.plane(0, sign) if axis == "x" else me.plane(sign, 0)
        return remote(block, block, send_sem.at[m], recv_sem.at[m], peer)

    def start_after(event):
        for m in sorted((m for m in range(len(messages)) if messages[m]["needs"] == event), key=lambda m: messages[m]["starts"]):
            copy_of(m, False).start()

    halo_copy = remote(grad_ref.at[pl.ds(0, TAPS)], halo, halo_sem.at[0], halo_sem.at[1], me.fsdp(-1))
    halo_copy.start()
    start_after("I")
    first[me.x, me.y] = convolve(toeplitz, grad_ref[...])
    start_after("B")
    halo_copy.wait_recv()
    tail = jnp.where(me.f == me.F - 1, jnp.zeros_like(halo[...]), halo[...])
    second[me.y, me.x] = convolve(toeplitz, jnp.concatenate([grad_ref[TAPS:, :], tail], axis=0))
    start_after("A")
    for m in order:
        copy_of(m, True).wait_recv()
        start_after(m)
    halo_copy.wait_send()
    for m in order:
        copy_of(m, False).wait_send()

    blended_ref[...] = momentum_ref[...]

    def add(f, carry):
        y, x = f // me.X, lax.rem(f, me.X)
        rows = jnp.concatenate([first[x, y], second[y, x]], axis=0)
        columns = pl.ds(pl.multiple_of(lax.rem(f, 2) * 2 * TAPS, 2 * TAPS), 2 * TAPS)
        blended_ref[...] += jnp.dot(features[f // 2, :, columns], rows, preferred_element_type=jnp.float32)
        return carry

    lax.fori_loop(0, me.F, add, 0)
    sketch_ref[...] = jnp.dot(blended_ref[...], basis_ref[...], precision=HIGHEST, preferred_element_type=jnp.float32)


def rows_dot(left, right):
    return lax.dot_general(
        left, right, (((0,), (0,)), ((), ())), precision=HIGHEST, preferred_element_type=jnp.float32
    )


def dot_t(left, right):
    return lax.dot_general(
        left, right, (((1,), (1,)), ((), ())), precision=HIGHEST, preferred_element_type=jnp.float32
    )


def dot(left, right):
    return jnp.dot(left, right, precision=HIGHEST, preferred_element_type=jnp.float32)


def sum_kernel(
    sizes, partial_ref, blended_ref, sketch_ref, gram_ref, right_ref,
    half_in, half_sum, z_in, gram_part, right_part, gram_in, right_in,
    core_sem, z_send, z_recv, f_send, f_recv,
):
    me = Place(sizes)
    peers = [me.sibling()] + [me.along_z(d) for d in range(1, me.Z)] + [me.fsdp(d) for d in range(1, me.F)]
    greet(peers)
    all_greeted(peers)
    half = partial_ref.shape[0] // 2
    mine = pl.ds(pl.multiple_of(me.c * half, 8), half)
    other = pl.ds(pl.multiple_of((1 - me.c) * half, 8), half)
    swap = remote(partial_ref.at[other], half_in, core_sem.at[0], core_sem.at[1], me.sibling())
    swap.start()
    swap.wait()
    half_sum[...] = partial_ref[mine, :] + half_in[...]
    piece = half // me.Z

    def z_rows(z, base):
        return pl.ds(pl.multiple_of(base + z * piece, 8), piece)

    out = []
    for d in range(1, me.Z):
        out.append(remote(half_sum.at[z_rows(me.wrap(me.z + d, me.Z), 0)], z_in.at[d], z_send.at[0, d], z_recv.at[0, d], me.along_z(d)))
        out[-1].start()
    total = half_sum[z_rows(me.z, 0), :]
    for d in range(1, me.Z):
        out[d - 1].wait_recv()
        total = total + z_in[d]
    held = z_rows(me.z, me.c * half)
    sketch_ref[held, :] = total
    for d in range(1, me.Z):
        out.append(remote(sketch_ref.at[held], sketch_ref.at[held], z_send.at[1, d], z_recv.at[1, d], me.along_z(d)))
        out[-1].start()
    for d in range(1, me.Z):
        there = sketch_ref.at[z_rows(me.wrap(me.z - d, me.Z), me.c * half)]
        remote(there, there, z_send.at[1, d], z_recv.at[1, d], me.along_z(d)).wait_recv()
    swap = remote(sketch_ref.at[mine], sketch_ref.at[mine], core_sem.at[2], core_sem.at[3], me.sibling())
    swap.start()
    swap.wait_send()
    remote(sketch_ref.at[other], sketch_ref.at[other], core_sem.at[2], core_sem.at[3], me.sibling()).wait_recv()
    sketch = sketch_ref[...]

    def scatter(kind, part, into):
        rows = part.shape[0] // me.F
        for d in range(1, me.F):
            there = pl.ds(pl.multiple_of(me.wrap(me.f + d, me.F) * rows, 8), rows)
            out.append(remote(part.at[there], into.at[d], f_send.at[kind, d], f_recv.at[kind, d], me.fsdp(d)))
            out[-1].start()

    def collect(kind, part, into, result):
        rows = part.shape[0] // me.F
        here = pl.ds(pl.multiple_of(me.f * rows, 8), rows)
        total = part[here, :]
        for d in range(1, me.F):
            remote(into.at[d], into.at[d], f_send.at[kind, d], f_recv.at[kind, d], me.fsdp(d)).wait_recv()
            total = total + into[d]
        result[here, :] = total
        for d in range(1, me.F):
            out.append(remote(result.at[here], result.at[here], f_send.at[kind + 1, d], f_recv.at[kind + 1, d], me.fsdp(d)))
            out[-1].start()

    def arrive(kind, result):
        rows = result.shape[0] // me.F
        for d in range(1, me.F):
            there = result.at[pl.ds(pl.multiple_of(me.wrap(me.f - d, me.F) * rows, 8), rows)]
            remote(there, there, f_send.at[kind, d], f_recv.at[kind, d], me.fsdp(d)).wait_recv()

    gram_part[...] = rows_dot(sketch, sketch)
    scatter(0, gram_part, gram_in)
    right_part[...] = rows_dot(blended_ref[...], sketch)
    scatter(2, right_part, right_in)
    collect(0, gram_part, gram_in, gram_ref)
    collect(2, right_part, right_in, right_ref)
    arrive(1, gram_ref)
    arrive(3, right_ref)
    for copy in out:
        copy.wait_send()


def inverse_factor(rows):
    shape = (8, 128)
    rows = list(rows)
    lane = lax.broadcasted_iota(jnp.int32, shape, 1)
    sub = lax.broadcasted_iota(jnp.int32, shape, 0)

    def column(value, k):
        return jnp.broadcast_to(value[:, k : k + 1], shape)

    def row(value, k):
        return jnp.broadcast_to(value[k : k + 1, :], shape)

    for b in range(len(rows)):
        base = 8 * b
        pivot = rows[b]
        columns = [column(pivot, base + j) for j in range(8)]
        inside = (lane >= base) & (lane < base + 8)
        pivot = jnp.where(inside, jnp.where(lane - base == sub, 1.0, 0.0), pivot)
        scale = jnp.zeros(shape, jnp.float32)
        inverses, uppers, crossed = [], [], {}
        for j in range(8):
            diagonal = row(columns[j], j)
            inverse = 1.0 / diagonal
            lower = jnp.where(sub > j, columns[j] * inverse, 0.0)
            scale = jnp.where(sub == j, lax.rsqrt(diagonal), scale)
            for k in range(j + 1, 8):
                crossed[j, k] = row(columns[k], j)
                columns[k] = columns[k] - lower * crossed[j, k]
            upper = row(pivot, j)
            pivot = pivot - lower * upper
            inverses.append(inverse)
            uppers.append(upper)
        rows[b] = jnp.where(lane < base + 8, pivot * scale, 0.0)
        for i in range(b + 1, len(rows)):
            below = rows[i]
            columns = [column(below, base + j) for j in range(8)]
            below = jnp.where(inside, 0.0, below)
            for j in range(8):
                lower = columns[j] * inverses[j]
                for k in range(j + 1, 8):
                    columns[k] = columns[k] - lower * crossed[j, k]
                below = below - lower * uppers[j]
            rows[i] = below
    return rows


def by_eight(block):
    return [block[8 * i : 8 * i + 8, :] for i in range(block.shape[0] // 8)]


def factor_kernel(gram_ref, inverse_ref):
    h = gram_ref.shape[0] // 2
    top = jnp.concatenate(inverse_factor(by_eight(gram_ref[:h, :h])), axis=0)
    lower = dot_t(gram_ref[h:, :h], top)
    rest = gram_ref[h:, h:] - dot_t(lower, lower)
    bottom = jnp.concatenate(inverse_factor(by_eight(rest)), axis=0)
    inverse_ref[:h, :h] = top
    inverse_ref[:h, h:] = jnp.zeros((h, h), jnp.float32)
    inverse_ref[h:, :h] = -dot(bottom, dot(lower, top))
    inverse_ref[h:, h:] = bottom


def finish_kernel(
    sizes, sketch_ref, right_ref, inverse_ref, blended_ref, update_ref, momentum_ref, basis_ref, squares, send_sem, recv_sem
):
    me = Place(sizes)
    peers = [me.tensor(d) for d in range(1, me.T)]
    greet(peers)
    inverse = inverse_ref[...]
    projected = dot_t(right_ref[...], inverse)
    squares[0] = jnp.sum(projected * projected, axis=0, keepdims=True)
    all_greeted(peers)
    out = []
    for d in range(1, me.T):
        out.append(remote(squares.at[0], squares.at[d], send_sem.at[d], recv_sem.at[d], me.tensor(d)))
        out[-1].start()
    orthonormal = dot_t(sketch_ref[...], inverse)
    momentum_ref[...] = blended_ref[...] - (1.0 - momentum_decay) * dot_t(orthonormal, projected)
    total = squares[0]
    for d in range(1, me.T):
        out[d - 1].wait_recv()
        total = total + squares[d]
    new_basis = projected / jnp.sqrt(total / D + epsilon)
    basis_ref[...] = new_basis
    update_ref[...] = (math.sqrt(D / RANK) * dot_t(orthonormal, new_basis)).astype(jnp.bfloat16)
    for copy in out:
        copy.wait_send()


def call(kernel, name, outs, scratch, collective, *args, flops=0):
    params = dict(vmem_limit_bytes=48 << 20)
    if collective is not None:
        params.update(collective_id=collective, has_side_effects=True)
    return pl.pallas_call(
        kernel,
        name=name,
        out_shape=[jax.ShapeDtypeStruct(shape, dtype) for shape, dtype in outs],
        in_specs=[VMEM] * len(args),
        out_specs=[VMEM] * len(outs),
        scratch_shapes=scratch,
        compiler_params=pltpu.CompilerParams(**params),
        cost_estimate=pl.CostEstimate(flops=flops, bytes_accessed=4 << 20, transcendentals=0),
    )(*args)


def shards(sizes, inputs, grad_out, filters, momentum, basis):
    X, Y, Z = sizes
    F, T = X * Y, 2 * Z
    dma = pltpu.SemaphoreType.DMA
    f32, bf16 = jnp.float32, jnp.bfloat16
    tokens, channels = grad_out.shape
    width = inputs.shape[1]
    messages, _, _ = plan(sizes)
    blended, partial = call(
        functools.partial(gather_kernel, sizes), "gather",
        [((width, channels), f32), ((width, RANK), f32)],
        [
            pltpu.VMEM((TAPS, channels), bf16),
            pltpu.VMEM((filters.shape[0] * TAPS, 2 * TAPS), bf16),
            pltpu.VMEM((X, Y, HALF, channels), bf16),
            pltpu.VMEM((Y, X, HALF, channels), bf16),
            pltpu.VMEM((T, width, inputs.shape[0]), bf16),
            dma((2,)), dma((len(messages),)), dma((len(messages),)),
        ],
        1, inputs, grad_out, filters, momentum, basis, flops=3 * 10**9,
    )
    half = width // 2
    sketch, gram, right = call(
        functools.partial(sum_kernel, sizes), "sums",
        [((width, RANK), f32), ((RANK, RANK), f32), ((channels, RANK), f32)],
        [
            pltpu.VMEM((half, RANK), f32), pltpu.VMEM((half, RANK), f32),
            pltpu.VMEM((Z, half // Z, RANK), f32),
            pltpu.VMEM((RANK, RANK), f32), pltpu.VMEM((channels, RANK), f32),
            pltpu.VMEM((F, RANK // F, RANK), f32), pltpu.VMEM((F, channels // F, RANK), f32),
            dma((4,)), dma((2, Z)), dma((2, Z)), dma((4, F)), dma((4, F)),
        ],
        2, partial, blended, flops=10**9,
    )
    (inverse,) = call(factor_kernel, "factor", [((RANK, RANK), f32)], [], None, gram, flops=10**9)
    return tuple(call(
        functools.partial(finish_kernel, sizes), "finish",
        [((width, channels), bf16), ((width, channels), f32), ((channels, RANK), f32)],
        [pltpu.VMEM((T, 1, RANK), f32), dma((T,)), dma((T,))],
        3, sketch, right, inverse, blended, flops=10**9,
    ))


def solution(mesh):
    fsdp, tensor = mesh.shape["fsdp"], mesh.shape["tensor"]
    X = 4 if fsdp == 32 else 2
    placed = (
        P("tensor", "fsdp"),
        P("fsdp", "tensor"),
        P("tensor", None),
        P("fsdp", "tensor"),
        P("tensor", None),
    )
    return jax.shard_map(
        functools.partial(shards, (X, fsdp // X, tensor // 2)),
        mesh=mesh,
        in_specs=placed,
        out_specs=(P("fsdp", "tensor"), P("fsdp", "tensor"), P("tensor", None)),
        check_vma=False,
    )
```

time: 795 us -> 165 us (0.21)
  waiting for transfers between devices: 536 us -> 0 us
  Pallas kernels: 0 us -> 157 us
  local copies, waits for them, and re-layouts: 134 us -> 6.96 us
  other arithmetic: 58.7 us -> 0 us
  blocking collectives: 29.2 us -> 0 us
  matrix products: 19 us -> 0 us
  between operations: 15.4 us -> 0.68 us
    psum x3 -> x0, waiting for transfers between devices: 423 us -> none  [the longest x1 156 us: shards(): projected = lax.psum(partial_right, 'fsdp')]
    pallas_call x0 -> x4, Pallas kernels: none -> 157 us  [call(): pl.pallas_call(kernel, name=name, out_shape=[jax.ShapeDtypeStruct(shape,...]
    gather x2 -> x0, local copies, waits for them, and re-layouts: 122 us -> none  [toeplitz(): picked = jnp.take(filters, jnp.clip(offset, 0, taps - 1), axis=1)]
    all_gather x2 -> x0, waiting for transfers between devices: 112 us -> none  [the longest x1 112 us: shards(): lax.all_gather(grad_mixed, 'fsdp', axis=0, tiled=True)]
    another operation x10 -> x0, other arithmetic: 54.3 us -> none  [the longest x7 34.6 us: orthonormalize(): factor = jnp.linalg.cholesky(gram_matrix)]
    psum x1 -> x0, blocking collectives: 29.2 us -> none  [shards(): squares = lax.psum(jnp.sum(projected * projected, axis=0), 'tensor')]
    dot_general x7 -> x0, matrix products: 17.6 us -> none  [the longest x1 6.9 us: shards(): lax.dot_general(input_cols, lax.all_gather(grad_mixed, 'fsdp', axis=0, ti...]
  transfers between devices with their start and end apart: 6 -> 0, of which waited for: 4 -> 0; matrix products, arithmetic and copies ran while one was open for 16% -> 0% of each run, Pallas kernels for 0% -> 0%
where the time goes in v1:
time: 165 us
  Pallas kernels  157 us (95%)
  local copies, waits for them, and re-layouts  6.96 us (4%)
    pallas_call x4, Pallas kernels, call(): pl.pallas_call(kernel, name=name, out_shape=[jax.ShapeDtypeStruct(shape,...  157 us
    unnamed x13, local copies, waits for them, and re-layouts  6.96 us

profile of v1, /device:TPU:1, one launch (start us, length us, event | category | flops | bytes accessed | tf_op | source)
XLA Modules:
  0.0 164.6 jit_solution(6745971637862825655)
XLA Ops:
  0.6 0.0 copy-start
  0.6 1.0 copy-done
  1.7 0.0 copy-start.1
  1.7 1.0 copy-done.1
  2.7 0.0 copy-start.2
  2.7 0.9 copy-done.2
  3.7 0.0 copy-start.3
  3.7 0.9 copy-done.3
  4.6 0.0 copy-start.4
  4.6 0.7 copy-done.4
  5.3 73.5 %gather.1 = (f32[256,512]{1,0:T(8,128)S(1)}, f32[256,256]{1,0:T(8,128)S(1)}) custom-call(bf16[512,256]{1,0:T(8,128)(2,1)S(1)} %copy-done.2, bf16[256,512]{1,0:T(8,128)(2,1)S(1)} %copy-done.3, bf16[32,128]{1,0:T(8,128)(2,1)S(1)} %copy-done.4, f32[256,512]{1,0:T(8,128)S(1)} %copy-done, f32[512,256]{1,0:T(8,128)S(1)} %copy-done.1), custom_call_target="tpu_custom_call" | custom-call | flops 3000000000 | bytes 4194304 | tf_op jit(solution)/shard_map/gather/pallas_call | solution.py:402
  78.8 63.7 %sums.1 = (f32[256,256]{1,0:T(8,128)S(1)}, f32[256,256]{1,0:T(8,128)S(1)}, f32[512,256]{1,0:T(8,128)S(1)}) custom-call(f32[256,256]{1,0:T(8,128)S(1)} %get-tuple-element.8.partial_ref, f32[256,512]{1,0:T(8,128)S(1)} %get-tuple-element.9.blended_ref), custom_call_target="tpu_custom_call" | custom-call | flops 1000000000 | bytes 4194304 | tf_op jit(solution)/shard_map/sums/pallas_call | solution.py:402
  142.5 9.0 %factor.1.inverse_ref = f32[256,256]{1,0:T(8,128)S(1)} custom-call(f32[256,256]{1,0:T(8,128)S(1)} %get-tuple-element.12.gram_ref), custom_call_target="tpu_custom_call" | custom-call | flops 1000000000 | bytes 4194304 | tf_op jit(solution)/shard_map/factor/pallas_call | solution.py:402
  151.5 10.8 %finish.1 = (bf16[256,512]{1,0:T(8,128)(2,1)S(1)}, f32[256,512]{1,0:T(8,128)S(1)}, f32[512,256]{1,0:T(8,128)S(1)}) custom-call(f32[256,256]{1,0:T(8,128)S(1)} %get-tuple-element.10.sketch_ref, f32[512,256]{1,0:T(8,128)S(1)} %get-tuple-element.11.right_ref, f32[256,256]{1,0:T(8,128)S(1)} %factor.1.inverse_ref, f32[256,512]{1,0:T(8,128)S(1)} %get-tuple-element.9.blended_ref), custom_call_target="tpu_custom_call" | custom-call | flops 1000000000 | bytes 4194304 | tf_op jit(solution)/shard_map/finish/pallas_call | solution.py:402
  162.3 0.7 copy.11
  163.0 0.8 copy.12
  163.8 0.8 copy.13
Async XLA Ops:
  0.6 1.0 copy-start
  1.7 1.0 copy-start.1
  2.7 0.9 copy-start.2
  3.7 0.9 copy-start.3
  4.6 0.7 copy-start.4

commit v2 on v1

v2 whole, which is shorter than its diff:
```python
import functools
import math

import jax
import jax.numpy as jnp
from jax import lax
from jax.experimental import pallas as pl
from jax.experimental.pallas import tpu as pltpu
from jax.sharding import PartitionSpec as P

D = 8192
GROUP = 16
RANK = 256
TAPS = 128
HALF = 128

WHEN = (7.5, 14.0, 29.5, 34.0, 40.0, 46.0, 47.5, 57.0)

momentum_decay = 0.95
epsilon = 1e-06

MESH = pl.DeviceIdType.MESH
HIGHEST = lax.Precision.HIGHEST
VMEM = pl.BlockSpec(memory_space=pltpu.VMEM)
ANY = pl.BlockSpec(memory_space=pl.ANY)


class Place:
    def __init__(self, sizes):
        self.X, self.Y, self.Z = sizes
        self.F, self.T = self.X * self.Y, self.Z * 2
        self.f, self.t = lax.axis_index("fsdp"), lax.axis_index("tensor")
        self.y, self.x = self.f // self.X, lax.rem(self.f, self.X)
        self.z, self.c = self.t // 2, lax.rem(self.t, 2)

    def wrap(self, value, n):
        return lax.rem(value + 2 * n, n)

    def plane(self, dy, dx):
        return (self.wrap(self.y + dy, self.Y) * self.X + self.wrap(self.x + dx, self.X), self.t)

    def along_z(self, dz):
        return (self.f, self.wrap(self.z + dz, self.Z) * 2 + self.c)

    def sibling(self):
        return (self.f, self.z * 2 + 1 - self.c)

    def fsdp(self, d):
        return (self.wrap(self.f + d, self.F), self.t)

    def tensor(self, d):
        return (self.f, self.wrap(self.t + d, self.T))


def greet(peers):
    barrier = pltpu.get_barrier_semaphore()
    for peer in peers:
        pl.semaphore_signal(barrier, inc=1, device_id=peer, device_id_type=MESH)


def all_greeted(peers):
    pl.semaphore_wait(pltpu.get_barrier_semaphore(), len(peers))


def remote(src, dst, send, recv, peer):
    return pltpu.make_async_remote_copy(
        src_ref=src, dst_ref=dst, send_sem=send, recv_sem=recv, device_id=peer, device_id_type=MESH
    )


def ring(n, axis, rows, tell, first):
    lo, count = rows
    half = n // 2
    pieces = [(0, rows, first)]
    for sign in (1, -1):
        before = first
        for step in range(1, half + 1):
            part = rows
            if step == half:
                part = (lo, count // 2) if sign > 0 else (lo + count // 2, count // 2)
            before = tell(axis, sign, sign * (step - 1), part, before)
            pieces.append((sign * step, part, before))
    return pieces


def plan(sizes):
    X, Y, Z = sizes
    messages = []

    def teller(part, fixed):
        def tell(axis, sign, offset, rows, needs):
            where = dict(fixed)
            where[axis] = offset
            messages.append(dict(part=part, axis=axis, sign=sign, at=where, rows=rows, needs=needs))
            return len(messages) - 1

        return tell

    for ox, rows, needs in ring(X, "x", (0, HALF), teller("A", {"y": 0}), "A"):
        ring(Y, "y", rows, teller("A", {"x": ox}), needs)
    for oy, rows, needs in ring(Y, "y", (0, HALF), teller("B", {"x": 0}), "B"):
        ring(X, "x", rows, teller("B", {"y": oy}), needs)
    for oz, rows, needs in ring(Z, "z", (0, 256), teller("I", {}), "I"):
        teller("I", {"z": oz})("c", 1, 0, rows, needs)
    ready = {"I": 0.3, "B": 2.5, "A": 5.5}
    free, arrival = {}, {}
    waiting = list(range(len(messages)))
    while waiting:
        when = {m: ready[messages[m]["needs"]] for m in waiting if messages[m]["needs"] in ready}
        best = min(when, key=lambda m: (max(when[m], free.get((messages[m]["axis"], messages[m]["sign"]), 0)), when[m], m))
        message = messages[best]
        link = (message["axis"], message["sign"])
        start = max(when[best], free.get(link, 0.0))
        length = message["rows"][1] * 1024 * (2 / 1e5 if link[0] != "c" else 1 / 4e5)
        free[link] = start + length
        ready[best] = arrival[best] = start + length + 1.8
        message["starts"] = start
        waiting.remove(best)
    order = sorted(arrival, key=lambda m: arrival[m])
    return messages, order, arrival


def strided_taps(filters, toeplitz_ref):
    shape = (TAPS, TAPS)
    upper = lax.broadcasted_iota(jnp.int32, shape, 1) >= lax.broadcasted_iota(jnp.int32, shape, 0)
    for g in range(filters.shape[0]):
        rolled = pltpu.roll(jnp.broadcast_to(filters[g : g + 1, :], shape), 0, 1, stride=1, stride_axis=0)
        rows = pl.ds(g * TAPS, TAPS)
        toeplitz_ref[rows, :TAPS] = jnp.where(upper, rolled, 0.0).astype(jnp.bfloat16)
        toeplitz_ref[rows, TAPS:] = jnp.where(upper, 0.0, rolled).astype(jnp.bfloat16)


def convolve(toeplitz_ref, window):
    channels = window.shape[1]
    group = lax.broadcasted_iota(jnp.int32, (TAPS, 128), 1) // GROUP
    each = 128 // GROUP
    columns = []
    for q in range(channels // 128):
        product = jnp.dot(
            toeplitz_ref[q * each * TAPS : (q + 1) * each * TAPS, :],
            window[:, q * 128 : (q + 1) * 128],
            preferred_element_type=jnp.float32,
        )
        total = product[:TAPS]
        for i in range(1, each):
            total = jnp.where(group == i, product[i * TAPS : (i + 1) * TAPS], total)
        columns.append(total)
    return jnp.concatenate(columns, axis=1).astype(jnp.bfloat16)


def rows_dot(left, right):
    return lax.dot_general(
        left, right, (((0,), (0,)), ((), ())), precision=HIGHEST, preferred_element_type=jnp.float32
    )


def dot_t(left, right):
    return lax.dot_general(
        left, right, (((1,), (1,)), ((), ())), precision=HIGHEST, preferred_element_type=jnp.float32
    )


def dot(left, right):
    return jnp.dot(left, right, precision=HIGHEST, preferred_element_type=jnp.float32)


def inverse_factor(rows):
    shape = (8, 128)
    rows = list(rows)
    lane = lax.broadcasted_iota(jnp.int32, shape, 1)
    sub = lax.broadcasted_iota(jnp.int32, shape, 0)

    def column(value, k):
        return jnp.broadcast_to(value[:, k : k + 1], shape)

    def row(value, k):
        return jnp.broadcast_to(value[k : k + 1, :], shape)

    for b in range(len(rows)):
        base = 8 * b
        pivot = rows[b]
        columns = [column(pivot, base + j) for j in range(8)]
        inside = (lane >= base) & (lane < base + 8)
        pivot = jnp.where(inside, jnp.where(lane - base == sub, 1.0, 0.0), pivot)
        scale = jnp.zeros(shape, jnp.float32)
        inverses, uppers, crossed = [], [], {}
        for j in range(8):
            diagonal = row(columns[j], j)
            inverse = 1.0 / diagonal
            lower = jnp.where(sub > j, columns[j] * inverse, 0.0)
            scale = jnp.where(sub == j, lax.rsqrt(diagonal), scale)
            for k in range(j + 1, 8):
                crossed[j, k] = row(columns[k], j)
                columns[k] = columns[k] - lower * crossed[j, k]
            upper = row(pivot, j)
            pivot = pivot - lower * upper
            inverses.append(inverse)
            uppers.append(upper)
        rows[b] = jnp.where(lane < base + 8, pivot * scale, 0.0)
        for i in range(b + 1, len(rows)):
            below = rows[i]
            columns = [column(below, base + j) for j in range(8)]
            below = jnp.where(inside, 0.0, below)
            for j in range(8):
                lower = columns[j] * inverses[j]
                for k in range(j + 1, 8):
                    columns[k] = columns[k] - lower * crossed[j, k]
                below = below - lower * uppers[j]
            rows[i] = below
    return rows


def by_eight(block):
    return [block[8 * i : 8 * i + 8, :] for i in range(block.shape[0] // 8)]


def in_three(value):
    high = value.astype(jnp.bfloat16)
    rest = value - high.astype(jnp.float32)
    middle = rest.astype(jnp.bfloat16)
    low = (rest - middle.astype(jnp.float32)).astype(jnp.bfloat16)
    return jnp.concatenate([high, middle, low], axis=1)


def three_dot(left, right):
    n = right.shape[1] // 3
    product = jnp.dot(left, right, preferred_element_type=jnp.float32)
    return product[:, :n] + (product[:, n : 2 * n] + product[:, 2 * n :])


def main_kernel(
    sizes, inputs_hbm, grad_hbm, filters_hbm, momentum_hbm, basis_hbm,
    orthonormal_ref, projected_ref, momentum_ref, scale_ref,
    inputs_ref, grad_ref, filters_ref, basis_ref, blended_ref,
    halo, toeplitz, first, second, features,
    mixed, mixed_in, mixed_half, mixed_z, mixed_all,
    partial, half_in, half_sum, z_in, sketch_ref,
    gram_part, gram_in, gram_all, right_part, right_in, right_ref, squares,
    load_sem, halo_sem, send_sem, recv_sem, core_sem, z_send, z_recv, f_send, f_recv, t_send, t_recv,
):
    me = Place(sizes)
    loads = [
        pltpu.make_async_copy(there, here, load_sem.at[i])
        for i, (there, here) in enumerate([
            (inputs_hbm, inputs_ref), (grad_hbm, grad_ref), (filters_hbm, filters_ref),
            (basis_hbm, basis_ref), (momentum_hbm, blended_ref),
        ])
    ]
    for load in loads:
        load.start()
    peers = [me.fsdp(d) for d in range(1, me.F)] + [me.tensor(d) for d in range(1, me.T)]
    greet(peers)
    messages, order, arrival = plan(sizes)
    loads[0].wait()
    features[me.t] = jnp.transpose(inputs_ref[...].astype(jnp.float32)).astype(jnp.bfloat16)
    loads[1].wait()
    all_greeted(peers)

    def copy_of(m, arriving):
        message = messages[m]
        sign = message["sign"]
        shift = sign if arriving else 0
        at, axis = dict(message["at"]), message["axis"]
        rows = pl.ds(*message["rows"])
        if axis in at:
            at[axis] += shift
        if message["part"] == "I":
            core = me.c
            if axis == "c" and arriving:
                core = 1 - me.c
            block = features.at[me.wrap(me.z - at["z"], me.Z) * 2 + core, rows]
            peer = me.sibling() if axis == "c" else me.along_z(sign)
        else:
            y, x = me.wrap(me.y - at["y"], me.Y), me.wrap(me.x - at["x"], me.X)
            block = second.at[y, x, rows] if message["part"] == "A" else first.at[x, y, rows]
            peer = me.plane(0, sign) if axis == "x" else me.plane(sign, 0)
        return remote(block, block, send_sem.at[m], recv_sem.at[m], peer)

    def start_after(event):
        for m in sorted((m for m in range(len(messages)) if messages[m]["needs"] == event), key=lambda m: messages[m]["starts"]):
            copy_of(m, False).start()

    def add(oy, ox):
        y, x = me.wrap(me.y - oy, me.Y), me.wrap(me.x - ox, me.X)
        f = y * me.X + x
        rows = jnp.concatenate([first[x, y], second[y, x]], axis=0)
        columns = pl.ds(pl.multiple_of(lax.rem(f, 2) * 2 * TAPS, 2 * TAPS), 2 * TAPS)
        blended_ref[...] += jnp.dot(features[f // 2, :, columns], rows, preferred_element_type=jnp.float32)

    have = {(part, 0, 0): HALF for part in "AB"}
    ready, pending = [(0, 0)], list(order)
    adding = []

    def features_here():
        return not any(messages[m]["part"] == "I" for m in pending)

    def pump(until):
        while pending and arrival[pending[0]] <= until:
            m = pending.pop(0)
            copy_of(m, True).wait_recv()
            start_after(m)
            message = messages[m]
            if message["part"] != "I":
                at = dict(message["at"])
                at[message["axis"]] += message["sign"]
                place = (at["y"] % me.Y, at["x"] % me.X)
                have[(message["part"],) + place] = have.get((message["part"],) + place, 0) + message["rows"][1]
                if have.get(("A",) + place) == HALF and have.get(("B",) + place) == HALF:
                    ready.append(place)
            if adding and features_here() and ready:
                add(*ready.pop(0))

    out = []

    def send(*args):
        out.append(remote(*args))
        out[-1].start()

    def drain():
        for copy in out:
            copy.wait_send()
        out.clear()

    send(grad_ref.at[pl.ds(0, TAPS)], halo, halo_sem.at[0], halo_sem.at[1], me.fsdp(-1))
    start_after("I")
    loads[2].wait()
    strided_taps(filters_ref[...].astype(jnp.float32), toeplitz)
    first[me.x, me.y] = convolve(toeplitz, grad_ref[...])
    start_after("B")
    loads[3].wait()
    basis_terms = in_three(basis_ref[...])
    mixed[:TAPS, :] = three_dot(first[me.x, me.y], basis_terms)
    out[0].wait_recv()
    tail = jnp.where(me.f == me.F - 1, jnp.zeros_like(halo[...]), halo[...])
    second[me.y, me.x] = convolve(toeplitz, jnp.concatenate([grad_ref[TAPS:, :], tail], axis=0))
    start_after("A")
    mixed[TAPS:, :] = three_dot(second[me.y, me.x], basis_terms)

    half = TAPS
    piece = half // me.Z
    mine = pl.ds(pl.multiple_of(me.c * half, 8), half)
    other = pl.ds(pl.multiple_of((1 - me.c) * half, 8), half)

    def z_rows(z, base):
        return pl.ds(pl.multiple_of(base + z * piece, 8), piece)

    def core_swap(kind, there, here):
        send(there, here, core_sem.at[kind, 0], core_sem.at[kind, 1], me.sibling())

    def core_here(kind, here):
        remote(here, here, core_sem.at[kind, 0], core_sem.at[kind, 1], me.sibling()).wait_recv()

    def z_scatter(kind, source, into):
        for d in range(1, me.Z):
            send(source.at[z_rows(me.wrap(me.z + d, me.Z), 0)], into.at[d], z_send.at[kind, d], z_recv.at[kind, d], me.along_z(d))

    def z_collect(kind, source, into):
        total = source[z_rows(me.z, 0), :]
        for d in range(1, me.Z):
            remote(into.at[d], into.at[d], z_send.at[kind, d], z_recv.at[kind, d], me.along_z(d)).wait_recv()
            total = total + into[d]
        return total

    def share(part, f):
        rows = part.shape[0] // me.F
        start = f * rows
        return part.at[pl.ds(start if len(part.shape) == 3 else pl.multiple_of(start, 8), rows)]

    def spread(kind, here):
        for d in range(1, me.F):
            send(here, here, f_send.at[kind, d], f_recv.at[kind, d], me.fsdp(d))

    def scatter(kind, part, into):
        for d in range(1, me.F):
            send(share(part, me.wrap(me.f + d, me.F)), into.at[d], f_send.at[kind, d], f_recv.at[kind, d], me.fsdp(d))

    def collect(kind, part, into, result):
        total = share(part, me.f)[...]
        for d in range(1, me.F):
            remote(into.at[d], into.at[d], f_send.at[kind, d], f_recv.at[kind, d], me.fsdp(d)).wait_recv()
            total = total + into[d]
        here = share(result, me.f)
        here[...] = total
        spread(kind + 1, here)

    def arrive(kind, result):
        for d in range(1, me.F):
            there = share(result, me.wrap(me.f - d, me.F))
            remote(there, there, f_send.at[kind, d], f_recv.at[kind, d], me.fsdp(d)).wait_recv()

    core_swap(0, mixed.at[other], mixed_in)
    loads[4].wait()
    partial[...] = dot(blended_ref[...], basis_ref[...])
    pump(WHEN[0])
    core_here(0, mixed_in)
    mixed_half[...] = mixed[mine, :] + mixed_in[...]
    z_scatter(0, mixed_half, mixed_z)
    pump(WHEN[1])
    own = mixed_all.at[pl.ds(me.f, 1)]
    own[0] = z_collect(0, mixed_half, mixed_z)
    spread(0, own)
    pump(WHEN[2])
    arrive(0, mixed_all)
    assert features_here()
    which = lax.broadcasted_iota(jnp.int32, (TAPS, 3 * RANK), 0) // piece

    def add_mixed(pair, carry):
        left, right = [], []
        for i in range(2):
            columns = pl.ds(pl.multiple_of(i * 2 * TAPS + me.c * TAPS, TAPS), TAPS)
            left.append(features[pair, :, columns])
            terms = in_three(mixed_all[2 * pair + i]).astype(jnp.float32)
            right.append(jnp.where(which == me.z, jnp.concatenate([terms] * me.Z, axis=0), 0.0).astype(jnp.bfloat16))
        partial[...] += three_dot(jnp.concatenate(left, axis=1), jnp.concatenate(right, axis=0))
        return carry

    lax.fori_loop(0, me.F // 2, add_mixed, 0)
    core_swap(1, partial.at[other], half_in)
    adding.append(True)
    pump(WHEN[3])
    core_here(1, half_in)
    half_sum[...] = partial[mine, :] + half_in[...]
    z_scatter(1, half_sum, z_in)
    pump(WHEN[4])
    held = z_rows(me.z, me.c * half)
    sketch_ref[held, :] = z_collect(1, half_sum, z_in)
    for d in range(1, me.Z):
        send(sketch_ref.at[held], sketch_ref.at[held], z_send.at[2, d], z_recv.at[2, d], me.along_z(d))
    pump(WHEN[5])
    for d in range(1, me.Z):
        there = sketch_ref.at[z_rows(me.wrap(me.z - d, me.Z), me.c * half)]
        remote(there, there, z_send.at[2, d], z_recv.at[2, d], me.along_z(d)).wait_recv()
    core_swap(2, sketch_ref.at[mine], sketch_ref.at[mine])
    pump(WHEN[6])
    core_here(2, sketch_ref.at[other])
    core_half = sketch_ref[:, pl.ds(pl.multiple_of(me.c * 128, 128), 128)]
    gram = rows_dot(core_half, sketch_ref[...])
    for i in range(16):
        for j in range(2):
            gram_part[2 * i + j] = gram[8 * i : 8 * i + 8, 128 * j : 128 * j + 128]
    scatter(1, gram_part, gram_in)
    pump(WHEN[7])
    gram_mine = gram_all.at[me.c]
    collect(1, gram_part, gram_in, gram_mine)
    pump(1e9)
    while ready:
        add(*ready.pop(0))
    right_part[...] = rows_dot(blended_ref[...], sketch_ref[...])
    scatter(3, right_part, right_in)
    for m in order:
        copy_of(m, False).wait_send()
    arrive(2, gram_mine)
    core_swap(3, gram_mine, gram_mine)
    core_here(3, gram_all.at[1 - me.c])

    top = jnp.concatenate(inverse_factor([gram_all[0, 2 * i] for i in range(16)]), axis=0)
    below = jnp.concatenate([gram_all[1, 2 * i] for i in range(16)], axis=0)
    lower = dot_t(below, top)
    rest = jnp.concatenate([gram_all[1, 2 * i + 1] for i in range(16)], axis=0) - dot_t(lower, lower)
    collect(3, right_part, right_in, right_ref)
    bottom = jnp.concatenate(inverse_factor(by_eight(rest)), axis=0)
    cross = -dot(bottom, dot(lower, top))
    inverse = jnp.concatenate([
        jnp.concatenate([top, jnp.zeros_like(top)], axis=1), jnp.concatenate([cross, bottom], axis=1)
    ], axis=0)
    arrive(4, right_ref)

    projected = dot_t(right_ref[...], inverse)
    projected_ref[...] = projected
    squares[0] = jnp.sum(projected * projected, axis=0, keepdims=True)
    for d in range(1, me.T):
        send(squares.at[0], squares.at[d], t_send.at[d], t_recv.at[d], me.tensor(d))
    orthonormal = dot_t(sketch_ref[...], inverse)
    orthonormal_ref[...] = orthonormal
    momentum_ref[...] = blended_ref[...] - (1.0 - momentum_decay) * dot_t(orthonormal, projected)
    total = squares[0]
    for d in range(1, me.T):
        remote(squares.at[d], squares.at[d], t_send.at[d], t_recv.at[d], me.tensor(d)).wait_recv()
        total = total + squares[d]
    scale_ref[...] = 1.0 / jnp.sqrt(total / D + epsilon)
    drain()


def finish_kernel(
    orthonormal_ref, projected_ref, momentum_ref, scale_ref, update_hbm, momentum_hbm, basis_hbm, update, basis, sems
):
    out = [pltpu.make_async_copy(momentum_ref, momentum_hbm, sems.at[0])]
    out[0].start()
    basis[...] = projected_ref[...] * scale_ref[...]
    out.append(pltpu.make_async_copy(basis, basis_hbm, sems.at[1]))
    out[1].start()
    update[...] = (math.sqrt(D / RANK) * dot_t(orthonormal_ref[...], basis[...])).astype(jnp.bfloat16)
    out.append(pltpu.make_async_copy(update, update_hbm, sems.at[2]))
    out[2].start()
    for copy in out:
        copy.wait()


def call(kernel, name, outs, scratch, collective, in_space, out_space, *args):
    params = dict(vmem_limit_bytes=56 << 20)
    if collective is not None:
        params.update(collective_id=collective, has_side_effects=True)
    return pl.pallas_call(
        kernel,
        name=name,
        out_shape=[jax.ShapeDtypeStruct(shape, dtype) for shape, dtype in outs],
        in_specs=[in_space] * len(args),
        out_specs=[out_space] * len(outs),
        scratch_shapes=scratch,
        compiler_params=pltpu.CompilerParams(**params),
        cost_estimate=pl.CostEstimate(flops=3 * 10**9, bytes_accessed=4 << 20, transcendentals=0),
    )(*args)


def shards(sizes, inputs, grad_out, filters, momentum, basis):
    X, Y, Z = sizes
    F, T = X * Y, 2 * Z
    dma = pltpu.SemaphoreType.DMA
    f32, bf16 = jnp.float32, jnp.bfloat16
    tokens, channels = grad_out.shape
    width = inputs.shape[1]
    messages, _, _ = plan(sizes)
    half = width // 2
    orthonormal, projected, momentum, scale = call(
        functools.partial(main_kernel, sizes), "main",
        [((width, RANK), f32), ((channels, RANK), f32), ((width, channels), f32), ((1, RANK), f32)],
        [
            pltpu.VMEM(inputs.shape, bf16), pltpu.VMEM(grad_out.shape, bf16), pltpu.VMEM(filters.shape, bf16),
            pltpu.VMEM(basis.shape, f32), pltpu.VMEM((width, channels), f32),
            pltpu.VMEM((TAPS, channels), bf16),
            pltpu.VMEM((filters.shape[0] * TAPS, 2 * TAPS), bf16),
            pltpu.VMEM((X, Y, HALF, channels), bf16),
            pltpu.VMEM((Y, X, HALF, channels), bf16),
            pltpu.VMEM((T, width, inputs.shape[0]), bf16),
            pltpu.VMEM((tokens, RANK), f32), pltpu.VMEM((TAPS, RANK), f32), pltpu.VMEM((TAPS, RANK), f32),
            pltpu.VMEM((Z, TAPS // Z, RANK), f32), pltpu.VMEM((F, TAPS // Z, RANK), f32),
            pltpu.VMEM((width, RANK), f32), pltpu.VMEM((half, RANK), f32), pltpu.VMEM((half, RANK), f32),
            pltpu.VMEM((Z, half // Z, RANK), f32), pltpu.VMEM((width, RANK), f32),
            pltpu.VMEM((32, 8, 128), f32), pltpu.VMEM((F, 32 // F, 8, 128), f32), pltpu.VMEM((2, 32, 8, 128), f32),
            pltpu.VMEM((channels, RANK), f32), pltpu.VMEM((F, channels // F, RANK), f32), pltpu.VMEM((channels, RANK), f32),
            pltpu.VMEM((T, 1, RANK), f32),
            dma((5,)), dma((2,)), dma((len(messages),)), dma((len(messages),)), dma((4, 2)),
            dma((3, Z)), dma((3, Z)), dma((5, F)), dma((5, F)), dma((T,)), dma((T,)),
        ],
        1, ANY, VMEM, inputs, grad_out, filters, momentum, basis,
    )
    return tuple(call(
        finish_kernel, "finish",
        [((width, channels), bf16), ((width, channels), f32), ((channels, RANK), f32)],
        [pltpu.VMEM((width, channels), bf16), pltpu.VMEM((channels, RANK), f32), dma((3,))],
        None, VMEM, ANY, orthonormal, projected, momentum, scale,
    ))


def solution(mesh):
    fsdp, tensor = mesh.shape["fsdp"], mesh.shape["tensor"]
    X = 4 if fsdp == 32 else 2
    placed = (
        P("tensor", "fsdp"),
        P("fsdp", "tensor"),
        P("tensor", None),
        P("fsdp", "tensor"),
        P("tensor", None),
    )
    return jax.shard_map(
        functools.partial(shards, (X, fsdp // X, tensor // 2)),
        mesh=mesh,
        in_specs=placed,
        out_specs=(P("fsdp", "tensor"), P("fsdp", "tensor"), P("tensor", None)),
        check_vma=False,
    )
```

time: 165 us -> 139 us (0.84)
  Pallas kernels: 157 us -> 138 us
  local copies, waits for them, and re-layouts: 6.96 us -> 0 us
    pallas_call x4 -> x2, Pallas kernels: 157 us -> 138 us  [call(): pl.pallas_call(kernel, name=name, out_shape=[jax.ShapeDtypeStruct(shape,...]
    unnamed x13 -> x0, local copies, waits for them, and re-layouts: 6.96 us -> none
where the time goes in v2:
time: 139 us; the launch traced here: 138 us
  Pallas kernels  138 us (99%)
    pallas_call x2, Pallas kernels, call(): pl.pallas_call(kernel, name=name, out_shape=[jax.ShapeDtypeStruct(shape,...  138 us

profile of v2, /device:TPU:1, one launch (start us, length us, event | category | flops | bytes accessed | tf_op | source)
XLA Modules:
  0.0 138.4 jit_solution(6396051263044998416)
XLA Ops:
  0.6 135.0 %main.1 = (f32[256,256]{1,0:T(8,128)}, f32[512,256]{1,0:T(8,128)}, f32[256,512]{1,0:T(8,128)}, f32[1,256]{1,0:T(1,128)}) custom-call(bf16[512,256]{1,0:T(8,128)(2,1)} %inputs_hbm.1, bf16[256,512]{1,0:T(8,128)(2,1)} %grad_hbm.1, bf16[32,128]{1,0:T(8,128)(2,1)} %filters_hbm.1, f32[256,512]{1,0:T(8,128)} %momentum_hbm.1, f32[512,256]{1,0:T(8,128)} %basis_hbm.1), custom_call_target="tpu_custom_call" | custom-call | flops 3000000000 | bytes 4194304 | tf_op jit(solution)/shard_map/main/pallas_call | solution.py:503
  135.6 2.7 %finish.1 = (bf16[256,512]{1,0:T(8,128)(2,1)}, f32[256,512]{1,0:T(8,128)}, f32[512,256]{1,0:T(8,128)}) custom-call(f32[256,256]{1,0:T(8,128)} %get-tuple-element.7.orthonormal_ref, f32[512,256]{1,0:T(8,128)} %get-tuple-element.8.projected_ref, f32[256,512]{1,0:T(8,128)} %get-tuple-element.9.momentum_ref, f32[1,256]{1,0:T(1,128)} %get-tuple-element.10.scale_ref), custom_call_target="tpu_custom_call" | custom-call | flops 3000000000 | bytes 4194304 | tf_op jit(solution)/shard_map/finish/pallas_call | solution.py:503

commit v3 on v2

--- a/solution.py
+++ b/solution.py
@@ -14,7 +14,7 @@
 TAPS = 128
 HALF = 128
 
-WHEN = (7.5, 14.0, 29.5, 34.0, 40.0, 46.0, 47.5, 57.0)
+WHEN = (10.0, 15.0, 21.0, 26.0, 33.0, 38.0, 39.5, 47.0, 52.0)
 
 momentum_decay = 0.95
 epsilon = 1e-06
@@ -96,8 +96,17 @@
 
         return tell
 
-    for ox, rows, needs in ring(X, "x", (0, HALF), teller("A", {"y": 0}), "A"):
-        ring(Y, "y", rows, teller("A", {"x": ox}), needs)
+    quarter = HALF // 4
+    for sign in (1, -1):
+        tell = teller("A", {"y": 0})
+        near = tell("x", sign, 0, (0, HALF), "A")
+        rows = (2 * quarter if sign > 0 else 3 * quarter, quarter)
+        ring(Y, "y", rows, teller("A", {"x": 2 * sign}), tell("x", sign, sign, rows, near))
+        for oy, rows, needs in ring(Y, "y", (0, HALF), teller("A", {"x": sign}), near):
+            if rows[0] == 0:
+                far = (0 if sign > 0 else quarter, quarter)
+                teller("A", {"y": oy})("x", sign, sign, far, needs)
+    ring(Y, "y", (0, HALF), teller("A", {"x": 0}), "A")
     for oy, rows, needs in ring(Y, "y", (0, HALF), teller("B", {"x": 0}), "B"):
         ring(X, "x", rows, teller("B", {"y": oy}), needs)
     for oz, rows, needs in ring(Z, "z", (0, 256), teller("I", {}), "I"):
@@ -234,9 +243,9 @@
     inputs_ref, grad_ref, filters_ref, basis_ref, blended_ref,
     halo, toeplitz, first, second, features,
     mixed, mixed_in, mixed_half, mixed_z, mixed_all,
-    partial, half_in, half_sum, z_in, sketch_ref,
-    gram_part, gram_in, gram_all, right_part, right_in, right_ref, squares,
-    load_sem, halo_sem, send_sem, recv_sem, core_sem, z_send, z_recv, f_send, f_recv, t_send, t_recv,
+    partial, half_in, half_sum, z_in, part, part_in, sketch_ref,
+    gram_part, gram_in, gram_all, right_part, right_x, right_mid, right_y, right_ref, squares,
+    load_sem, halo_sem, send_sem, recv_sem, core_sem, z_send, z_recv, f_send, f_recv, p_send, p_recv, t_send, t_recv,
 ):
     me = Place(sizes)
     loads = [
@@ -307,8 +316,9 @@
                 have[(message["part"],) + place] = have.get((message["part"],) + place, 0) + message["rows"][1]
                 if have.get(("A",) + place) == HALF and have.get(("B",) + place) == HALF:
                     ready.append(place)
-            if adding and features_here() and ready:
-                add(*ready.pop(0))
+            for _ in range(2):
+                if adding and features_here() and ready:
+                    add(*ready.pop(0))
 
     out = []
 
@@ -328,21 +338,24 @@
     first[me.x, me.y] = convolve(toeplitz, grad_ref[...])
     start_after("B")
     loads[3].wait()
-    basis_terms = in_three(basis_ref[...])
-    mixed[:TAPS, :] = three_dot(first[me.x, me.y], basis_terms)
+    basis_terms = in_three(jnp.transpose(basis_ref[...]))
+
+    def times_basis(rows):
+        product = 0.0
+        for i in range(3):
+            term = basis_terms[:, i * rows.shape[1] : (i + 1) * rows.shape[1]]
+            product += lax.dot_general(term, rows, (((1,), (1,)), ((), ())), preferred_element_type=jnp.float32)
+        return product
+
+    mixed[0] = times_basis(first[me.x, me.y])
     out[0].wait_recv()
     tail = jnp.where(me.f == me.F - 1, jnp.zeros_like(halo[...]), halo[...])
     second[me.y, me.x] = convolve(toeplitz, jnp.concatenate([grad_ref[TAPS:, :], tail], axis=0))
     start_after("A")
-    mixed[TAPS:, :] = three_dot(second[me.y, me.x], basis_terms)
-
-    half = TAPS
-    piece = half // me.Z
-    mine = pl.ds(pl.multiple_of(me.c * half, 8), half)
-    other = pl.ds(pl.multiple_of((1 - me.c) * half, 8), half)
-
-    def z_rows(z, base):
-        return pl.ds(pl.multiple_of(base + z * piece, 8), piece)
+    mixed[1] = times_basis(second[me.y, me.x])
+
+    piece = RANK // me.Z
+    small = piece // 2
 
     def core_swap(kind, there, here):
         send(there, here, core_sem.at[kind, 0], core_sem.at[kind, 1], me.sibling())
@@ -352,10 +365,10 @@
 
     def z_scatter(kind, source, into):
         for d in range(1, me.Z):
-            send(source.at[z_rows(me.wrap(me.z + d, me.Z), 0)], into.at[d], z_send.at[kind, d], z_recv.at[kind, d], me.along_z(d))
+            send(source.at[me.wrap(me.z + d, me.Z)], into.at[d], z_send.at[kind, d], z_recv.at[kind, d], me.along_z(d))
 
     def z_collect(kind, source, into):
-        total = source[z_rows(me.z, 0), :]
+        total = source[me.z]
         for d in range(1, me.Z):
             remote(into.at[d], into.at[d], z_send.at[kind, d], z_recv.at[kind, d], me.along_z(d)).wait_recv()
             total = total + into[d]
@@ -366,113 +379,188 @@
         start = f * rows
         return part.at[pl.ds(start if len(part.shape) == 3 else pl.multiple_of(start, 8), rows)]
 
-    def spread(kind, here):
-        for d in range(1, me.F):
-            send(here, here, f_send.at[kind, d], f_recv.at[kind, d], me.fsdp(d))
-
     def scatter(kind, part, into):
         for d in range(1, me.F):
             send(share(part, me.wrap(me.f + d, me.F)), into.at[d], f_send.at[kind, d], f_recv.at[kind, d], me.fsdp(d))
 
-    def collect(kind, part, into, result):
+    def collect(kind, part, into):
         total = share(part, me.f)[...]
         for d in range(1, me.F):
             remote(into.at[d], into.at[d], f_send.at[kind, d], f_recv.at[kind, d], me.fsdp(d)).wait_recv()
             total = total + into[d]
-        here = share(result, me.f)
-        here[...] = total
-        spread(kind + 1, here)
-
-    def arrive(kind, result):
-        for d in range(1, me.F):
-            there = share(result, me.wrap(me.f - d, me.F))
-            remote(there, there, f_send.at[kind, d], f_recv.at[kind, d], me.fsdp(d)).wait_recv()
-
-    core_swap(0, mixed.at[other], mixed_in)
+        return total
+
+
+    def gather_y(kind, block):
+        here = block(me.y, me.x)
+        for dy in range(1, me.Y):
+            send(here, here, p_send.at[kind, 0, dy], p_recv.at[kind, 0, dy], me.plane(dy, 0))
+        for dx in range(1, me.X):
+            send(here, here, p_send.at[kind, dx, 0], p_recv.at[kind, dx, 0], me.plane(0, dx))
+
+    def gather_x(kind, block):
+        for dy in sorted(range(1, me.Y), key=lambda d: min(d, me.Y - d)):
+            there = block(me.wrap(me.y - dy, me.Y), me.x)
+            remote(there, there, p_send.at[kind, 0, dy], p_recv.at[kind, 0, dy], me.plane(dy, 0)).wait_recv()
+            for dx in range(1, me.X):
+                send(there, there, p_send.at[kind, dx, dy], p_recv.at[kind, dx, dy], me.plane(0, dx))
+
+    def gathered(kind, block, columns=None):
+        for dx in columns or range(1, me.X):
+            for dy in range(me.Y):
+                there = block(me.wrap(me.y - dy, me.Y), me.wrap(me.x - dx, me.X))
+                remote(there, there, p_send.at[kind, dx, dy], p_recv.at[kind, dx, dy], me.plane(0, dx)).wait_recv()
+
+    core_swap(0, mixed.at[1 - me.c], mixed_in)
     loads[4].wait()
-    partial[...] = dot(blended_ref[...], basis_ref[...])
+    from_momentum = lax.dot_general(
+        jnp.transpose(basis_ref[...]), blended_ref[...], (((1,), (1,)), ((), ())),
+        precision=HIGHEST, preferred_element_type=jnp.float32,
+    )
+    for z in range(me.Z):
+        for c in range(2):
+            at = z * piece + c * small
+            partial[c, z] = from_momentum[at : at + small, :]
+    core_here(0, mixed_in)
+    for z in range(me.Z):
+        rows = slice(z * piece, (z + 1) * piece)
+        mixed_half[z] = mixed[me.c, rows, :] + mixed_in[rows, :]
+    z_scatter(0, mixed_half, mixed_z)
+    core_swap(1, partial.at[1 - me.c], half_in)
     pump(WHEN[0])
-    core_here(0, mixed_in)
-    mixed_half[...] = mixed[mine, :] + mixed_in[...]
-    z_scatter(0, mixed_half, mixed_z)
+    core_here(1, half_in)
+    half_sum[...] = partial[me.c] + half_in[...]
     pump(WHEN[1])
-    own = mixed_all.at[pl.ds(me.f, 1)]
-    own[0] = z_collect(0, mixed_half, mixed_z)
-    spread(0, own)
+    mixed_all[me.f] = z_collect(0, mixed_half, mixed_z)
+
+    def mixed_block(y, x):
+        return mixed_all.at[y * me.X + x]
+
+    gather_y(0, mixed_block)
+    z_scatter(1, half_sum, z_in)
     pump(WHEN[2])
-    arrive(0, mixed_all)
-    assert features_here()
-    which = lax.broadcasted_iota(jnp.int32, (TAPS, 3 * RANK), 0) // piece
-
-    def add_mixed(pair, carry):
-        left, right = [], []
-        for i in range(2):
-            columns = pl.ds(pl.multiple_of(i * 2 * TAPS + me.c * TAPS, TAPS), TAPS)
-            left.append(features[pair, :, columns])
-            terms = in_three(mixed_all[2 * pair + i]).astype(jnp.float32)
-            right.append(jnp.where(which == me.z, jnp.concatenate([terms] * me.Z, axis=0), 0.0).astype(jnp.bfloat16))
-        partial[...] += three_dot(jnp.concatenate(left, axis=1), jnp.concatenate(right, axis=0))
-        return carry
-
-    lax.fori_loop(0, me.F // 2, add_mixed, 0)
-    core_swap(1, partial.at[other], half_in)
+    gather_x(0, mixed_block)
+    pump(WHEN[3])
+    held = z_collect(1, half_sum, z_in)
+    gathered(0, mixed_block)
+    while not features_here():
+        pump(arrival[pending[0]])
+
+    def add_mixed(pair, total):
+        left = jnp.concatenate([mixed_all[2 * pair], mixed_all[2 * pair + 1]], axis=1)
+        high = left.astype(jnp.bfloat16)
+        rest = left - high.astype(jnp.float32)
+        middle = rest.astype(jnp.bfloat16)
+        low = (rest - middle.astype(jnp.float32)).astype(jnp.bfloat16)
+        columns = [pl.ds(pl.multiple_of(i * 2 * TAPS + me.c * TAPS, TAPS), TAPS) for i in range(2)]
+        right = jnp.concatenate([features[pair, :, column] for column in columns], axis=1)
+        return total + lax.dot_general(
+            jnp.concatenate([high, middle, low], axis=0), right, (((1,), (1,)), ((), ())), preferred_element_type=jnp.float32
+        )
+
+    total = lax.fori_loop(0, me.F // 2, add_mixed, jnp.zeros((3 * piece, features.shape[1]), jnp.float32))
+    total = total[:piece] + (total[piece : 2 * piece] + total[2 * piece :])
+    part[0] = total[:small]
+    part[1] = total[small:]
+    core_swap(2, part.at[1 - me.c], part_in)
     adding.append(True)
-    pump(WHEN[3])
-    core_here(1, half_in)
-    half_sum[...] = partial[mine, :] + half_in[...]
-    z_scatter(1, half_sum, z_in)
     pump(WHEN[4])
-    held = z_rows(me.z, me.c * half)
-    sketch_ref[held, :] = z_collect(1, half_sum, z_in)
+    core_here(2, part_in)
+    own = sketch_ref.at[me.c, me.z]
+    own[...] = held + (part[me.c] + part_in[...])
     for d in range(1, me.Z):
-        send(sketch_ref.at[held], sketch_ref.at[held], z_send.at[2, d], z_recv.at[2, d], me.along_z(d))
+        send(own, own, z_send.at[2, d], z_recv.at[2, d], me.along_z(d))
     pump(WHEN[5])
     for d in range(1, me.Z):
-        there = sketch_ref.at[z_rows(me.wrap(me.z - d, me.Z), me.c * half)]
+        there = sketch_ref.at[me.c, me.wrap(me.z - d, me.Z)]
         remote(there, there, z_send.at[2, d], z_recv.at[2, d], me.along_z(d)).wait_recv()
-    core_swap(2, sketch_ref.at[mine], sketch_ref.at[mine])
+    core_swap(3, sketch_ref.at[me.c], sketch_ref.at[me.c])
     pump(WHEN[6])
-    core_here(2, sketch_ref.at[other])
-    core_half = sketch_ref[:, pl.ds(pl.multiple_of(me.c * 128, 128), 128)]
-    gram = rows_dot(core_half, sketch_ref[...])
-    for i in range(16):
-        for j in range(2):
-            gram_part[2 * i + j] = gram[8 * i : 8 * i + 8, 128 * j : 128 * j + 128]
-    scatter(1, gram_part, gram_in)
+    core_here(3, sketch_ref.at[1 - me.c])
+    sketch_t = jnp.concatenate([sketch_ref[c, z] for z in range(me.Z) for c in range(2)], axis=0)
+    gram = dot_t(sketch_t, sketch_t)
+    for c in range(2):
+        @pl.when(me.c == c)
+        def _():
+            for i in range(16):
+                for j in range(2):
+                    at = 128 * c + 8 * i
+                    gram_part[2 * i + j] = gram[at : at + 8, 128 * j : 128 * j + 128]
+    scatter(0, gram_part, gram_in)
+    sketch = jnp.transpose(sketch_t)
     pump(WHEN[7])
     gram_mine = gram_all.at[me.c]
-    collect(1, gram_part, gram_in, gram_mine)
+
+    def gram_block(y, x):
+        return share(gram_mine, y * me.X + x)
+
+    gram_block(me.y, me.x)[...] = collect(0, gram_part, gram_in)
+    gather_y(3, gram_block)
+    pump(WHEN[8])
+    gather_x(3, gram_block)
     pump(1e9)
     while ready:
         add(*ready.pop(0))
-    right_part[...] = rows_dot(blended_ref[...], sketch_ref[...])
-    scatter(3, right_part, right_in)
+    right_part[...] = rows_dot(blended_ref[...], sketch)
+    column = right_part.shape[0] // me.X
+    block_rows = column // me.Y
+
+    def right_column(x):
+        return pl.ds(pl.multiple_of(x * column, 8), column)
+
+    def right_block(y, x):
+        return right_ref.at[pl.ds(pl.multiple_of(x * column + y * block_rows, 8), block_rows)]
+
+    for dx in range(1, me.X):
+        send(right_part.at[right_column(me.wrap(me.x + dx, me.X))], right_x.at[dx], p_send.at[1, dx, 0], p_recv.at[1, dx, 0], me.plane(0, dx))
     for m in order:
         copy_of(m, False).wait_send()
-    arrive(2, gram_mine)
-    core_swap(3, gram_mine, gram_mine)
-    core_here(3, gram_all.at[1 - me.c])
+    gathered(3, gram_block)
+    core_swap(4, gram_mine, gram_mine)
+    total = right_part[right_column(me.x), :]
+    for dx in range(1, me.X):
+        remote(right_x.at[dx], right_x.at[dx], p_send.at[1, dx, 0], p_recv.at[1, dx, 0], me.plane(0, dx)).wait_recv()
+        total = total + right_x[dx]
+    right_mid[...] = total
+
+    def middle_rows(y):
+        return pl.ds(pl.multiple_of(y * block_rows, 8), block_rows)
+
+    for dy in range(1, me.Y):
+        send(right_mid.at[middle_rows(me.wrap(me.y + dy, me.Y))], right_y.at[dy], p_send.at[1, 0, dy], p_recv.at[1, 0, dy], me.plane(dy, 0))
+    core_here(4, gram_all.at[1 - me.c])
 
     top = jnp.concatenate(inverse_factor([gram_all[0, 2 * i] for i in range(16)]), axis=0)
+    total = right_mid[middle_rows(me.y), :]
+    for dy in range(1, me.Y):
+        remote(right_y.at[dy], right_y.at[dy], p_send.at[1, 0, dy], p_recv.at[1, 0, dy], me.plane(dy, 0)).wait_recv()
+        total = total + right_y[dy]
+    right_block(me.y, me.x)[...] = total
+    gather_y(2, right_block)
     below = jnp.concatenate([gram_all[1, 2 * i] for i in range(16)], axis=0)
     lower = dot_t(below, top)
     rest = jnp.concatenate([gram_all[1, 2 * i + 1] for i in range(16)], axis=0) - dot_t(lower, lower)
-    collect(3, right_part, right_in, right_ref)
     bottom = jnp.concatenate(inverse_factor(by_eight(rest)), axis=0)
+    gather_x(2, right_block)
     cross = -dot(bottom, dot(lower, top))
     inverse = jnp.concatenate([
         jnp.concatenate([top, jnp.zeros_like(top)], axis=1), jnp.concatenate([cross, bottom], axis=1)
     ], axis=0)
-    arrive(4, right_ref)
-
-    projected = dot_t(right_ref[...], inverse)
-    projected_ref[...] = projected
-    squares[0] = jnp.sum(projected * projected, axis=0, keepdims=True)
+    orthonormal = dot_t(sketch, inverse)
+    orthonormal_ref[...] = orthonormal
+    drain()
+    total = 0.0
+    for dx in sorted(range(me.X), key=lambda d: min(d, me.X - d)):
+        if dx:
+            gathered(2, right_block, [dx])
+        rows = right_column(me.wrap(me.x - dx, me.X))
+        projected = dot_t(right_ref[rows, :], inverse)
+        projected_ref[rows, :] = projected
+        total += jnp.sum(projected * projected, axis=0, keepdims=True)
+    squares[0] = total
     for d in range(1, me.T):
         send(squares.at[0], squares.at[d], t_send.at[d], t_recv.at[d], me.tensor(d))
-    orthonormal = dot_t(sketch_ref[...], inverse)
-    orthonormal_ref[...] = orthonormal
-    momentum_ref[...] = blended_ref[...] - (1.0 - momentum_decay) * dot_t(orthonormal, projected)
+    momentum_ref[...] = blended_ref[...] - (1.0 - momentum_decay) * dot_t(orthonormal, projected_ref[...])
     total = squares[0]
     for d in range(1, me.T):
         remote(squares.at[d], squares.at[d], t_send.at[d], t_recv.at[d], me.tensor(d)).wait_recv()
@@ -520,7 +608,6 @@
     tokens, channels = grad_out.shape
     width = inputs.shape[1]
     messages, _, _ = plan(sizes)
-    half = width // 2
     orthonormal, projected, momentum, scale = call(
         functools.partial(main_kernel, sizes), "main",
         [((width, RANK), f32), ((channels, RANK), f32), ((width, channels), f32), ((1, RANK), f32)],
@@ -532,15 +619,17 @@
             pltpu.VMEM((X, Y, HALF, channels), bf16),
             pltpu.VMEM((Y, X, HALF, channels), bf16),
             pltpu.VMEM((T, width, inputs.shape[0]), bf16),
-            pltpu.VMEM((tokens, RANK), f32), pltpu.VMEM((TAPS, RANK), f32), pltpu.VMEM((TAPS, RANK), f32),
-            pltpu.VMEM((Z, TAPS // Z, RANK), f32), pltpu.VMEM((F, TAPS // Z, RANK), f32),
-            pltpu.VMEM((width, RANK), f32), pltpu.VMEM((half, RANK), f32), pltpu.VMEM((half, RANK), f32),
-            pltpu.VMEM((Z, half // Z, RANK), f32), pltpu.VMEM((width, RANK), f32),
+            pltpu.VMEM((2, RANK, TAPS), f32), pltpu.VMEM((RANK, TAPS), f32), pltpu.VMEM((Z, RANK // Z, TAPS), f32),
+            pltpu.VMEM((Z, RANK // Z, TAPS), f32), pltpu.VMEM((F, RANK // Z, TAPS), f32),
+            pltpu.VMEM((2, Z, RANK // T, width), f32), pltpu.VMEM((Z, RANK // T, width), f32),
+            pltpu.VMEM((Z, RANK // T, width), f32), pltpu.VMEM((Z, RANK // T, width), f32),
+            pltpu.VMEM((2, RANK // T, width), f32), pltpu.VMEM((RANK // T, width), f32), pltpu.VMEM((2, Z, RANK // T, width), f32),
             pltpu.VMEM((32, 8, 128), f32), pltpu.VMEM((F, 32 // F, 8, 128), f32), pltpu.VMEM((2, 32, 8, 128), f32),
-            pltpu.VMEM((channels, RANK), f32), pltpu.VMEM((F, channels // F, RANK), f32), pltpu.VMEM((channels, RANK), f32),
+            pltpu.VMEM((channels, RANK), f32), pltpu.VMEM((X, channels // X, RANK), f32), pltpu.VMEM((channels // X, RANK), f32),
+            pltpu.VMEM((Y, channels // F, RANK), f32), pltpu.VMEM((channels, RANK), f32),
             pltpu.VMEM((T, 1, RANK), f32),
-            dma((5,)), dma((2,)), dma((len(messages),)), dma((len(messages),)), dma((4, 2)),
-            dma((3, Z)), dma((3, Z)), dma((5, F)), dma((5, F)), dma((T,)), dma((T,)),
+            dma((5,)), dma((2,)), dma((len(messages),)), dma((len(messages),)), dma((5, 2)),
+            dma((3, Z)), dma((3, Z)), dma((1, F)), dma((1, F)), dma((4, X, Y)), dma((4, X, Y)), dma((T,)), dma((T,)),
         ],
         1, ANY, VMEM, inputs, grad_out, filters, momentum, basis,
     )

time: 139 us -> 123 us (0.88)
  Pallas kernels: 138 us -> 122 us
    pallas_call x2, Pallas kernels: 138 us -> 122 us  [call(): pl.pallas_call(kernel, name=name, out_shape=[jax.ShapeDtypeStruct(shape,...]
where the time goes in v3:
time: 123 us
  Pallas kernels  122 us (99%)
    pallas_call x2, Pallas kernels, call(): pl.pallas_call(kernel, name=name, out_shape=[jax.ShapeDtypeStruct(shape,...  122 us

profile of v3, /device:TPU:1, one launch (start us, length us, event | category | flops | bytes accessed | tf_op | source)
XLA Modules:
  0.0 122.6 jit_solution(16136880729558163019)
XLA Ops:
  0.6 119.1 %main.1 = (f32[256,256]{1,0:T(8,128)}, f32[512,256]{1,0:T(8,128)}, f32[256,512]{1,0:T(8,128)}, f32[1,256]{1,0:T(1,128)}) custom-call(bf16[512,256]{1,0:T(8,128)(2,1)} %inputs_hbm.1, bf16[256,512]{1,0:T(8,128)(2,1)} %grad_hbm.1, bf16[32,128]{1,0:T(8,128)(2,1)} %filters_hbm.1, f32[256,512]{1,0:T(8,128)} %momentum_hbm.1, f32[512,256]{1,0:T(8,128)} %basis_hbm.1), custom_call_target="tpu_custom_call" | custom-call | flops 3000000000 | bytes 4194304 | tf_op jit(solution)/shard_map/main/pallas_call | solution.py:591
  119.8 2.7 %finish.1 = (bf16[256,512]{1,0:T(8,128)(2,1)}, f32[256,512]{1,0:T(8,128)}, f32[512,256]{1,0:T(8,128)}) custom-call(f32[256,256]{1,0:T(8,128)} %get-tuple-element.7.orthonormal_ref, f32[512,256]{1,0:T(8,128)} %get-tuple-element.8.projected_ref, f32[256,512]{1,0:T(8,128)} %get-tuple-element.9.momentum_ref, f32[1,256]{1,0:T(1,128)} %get-tuple-element.10.scale_ref), custom_call_target="tpu_custom_call" | custom-call | flops 3000000000 | bytes 4194304 | tf_op jit(solution)/shard_map/finish/pallas_call | solution.py:591

commit v4 on v3

--- a/solution.py
+++ b/solution.py
@@ -109,8 +109,9 @@
     ring(Y, "y", (0, HALF), teller("A", {"x": 0}), "A")
     for oy, rows, needs in ring(Y, "y", (0, HALF), teller("B", {"x": 0}), "B"):
         ring(X, "x", rows, teller("B", {"y": oy}), needs)
-    for oz, rows, needs in ring(Z, "z", (0, 256), teller("I", {}), "I"):
-        teller("I", {"z": oz})("c", 1, 0, rows, needs)
+    for lo in (0, 128):
+        for oz, rows, needs in ring(Z, "z", (lo, 128), teller("I", {}), "I"):
+            teller("I", {"z": oz})("c", 1, 0, rows, needs)
     ready = {"I": 0.3, "B": 2.5, "A": 5.5}
     free, arrival = {}, {}
     waiting = list(range(len(messages)))

time: 123 us -> 124 us (level)
    pallas_call x2, Pallas kernels: 122 us -> 123 us  [call(): pl.pallas_call(kernel, name=name, out_shape=[jax.ShapeDtypeStruct(shape,...]
where the time goes in v4:
time: 124 us
  Pallas kernels  123 us (99%)
    pallas_call x2, Pallas kernels, call(): pl.pallas_call(kernel, name=name, out_shape=[jax.ShapeDtypeStruct(shape,...  123 us

profile of v4, /device:TPU:1, one launch (start us, length us, event | category | flops | bytes accessed | tf_op | source)
XLA Modules:
  0.0 123.8 jit_solution(2590242283073290132)
XLA Ops:
  0.6 120.4 %main.1 = (f32[256,256]{1,0:T(8,128)}, f32[512,256]{1,0:T(8,128)}, f32[256,512]{1,0:T(8,128)}, f32[1,256]{1,0:T(1,128)}) custom-call(bf16[512,256]{1,0:T(8,128)(2,1)} %inputs_hbm.1, bf16[256,512]{1,0:T(8,128)(2,1)} %grad_hbm.1, bf16[32,128]{1,0:T(8,128)(2,1)} %filters_hbm.1, f32[256,512]{1,0:T(8,128)} %momentum_hbm.1, f32[512,256]{1,0:T(8,128)} %basis_hbm.1), custom_call_target="tpu_custom_call" | custom-call | flops 3000000000 | bytes 4194304 | tf_op jit(solution)/shard_map/main/pallas_call | solution.py:592
  121.0 2.7 %finish.1 = (bf16[256,512]{1,0:T(8,128)(2,1)}, f32[256,512]{1,0:T(8,128)}, f32[512,256]{1,0:T(8,128)}) custom-call(f32[256,256]{1,0:T(8,128)} %get-tuple-element.7.orthonormal_ref, f32[512,256]{1,0:T(8,128)} %get-tuple-element.8.projected_ref, f32[256,512]{1,0:T(8,128)} %get-tuple-element.9.momentum_ref, f32[1,256]{1,0:T(1,128)} %get-tuple-element.10.scale_ref), custom_call_target="tpu_custom_call" | custom-call | flops 3000000000 | bytes 4194304 | tf_op jit(solution)/shard_map/finish/pallas_call | solution.py:592
